TPU v7x, 32 devices: a whole 2x2x4 slice. The times are simulated.
32 devices in a mesh: dp: 8 (over y, x, core), tensor: 4 (over z).
Axes of the slice: x: 2, y: 2, z: 4, core: 2. Of those that a mesh axis runs over, the one named last changes fastest.
Arguments:
- d_out: bfloat16 [8, 512, 2560], P('dp', 'tensor'), may hold values from -12 to 12
- attn_out: bfloat16 [8, 512, 3072], P('dp', None, 'tensor'), may hold values from -6 to 6
- queries: bfloat16 [8, 512, 3072], P('dp', None, 'tensor'), may hold values from -40 to 40
- keys: bfloat16 [8, 512, 3072], P('dp', None, 'tensor'), may hold values from -4 to 4
- out_weight: bfloat16 [3072, 2560], P('tensor'), may hold values from -0.125 to 0.125
- segment_ids: int32 [8, 512], P('dp'), may hold values from 0 to 1, as said below
Outputs:
- value_grad: bfloat16 [8, 512, 3072], P('dp', None, 'tensor')
- weight_grad: float32 [3072, 2560], P(('tensor', 'dp'))
Inputs may be any that keep to these rules, and one draw needn't show every extreme that they name: `segment_ids`: ids start at 0, never fall along a sequence, and rise by one where a new document begins; exactly one new document begins in every aligned block of min(512, 512) positions.
All inputs are finite; a program needn't handle non-finite values.
Results may differ from a plain program's by a relative error of at most 0.008.
Values may be sent and summed in bfloat16 or wider, within the bound.
A program may use at most 64 MiB of HBM per device.

v0:
```python
import jax
import jax.numpy as jnp
from jax import lax
from jax.sharding import PartitionSpec as P

HEAD_DIM = 128


def value_path(queries, keys, attn_grad, segment_row):
    length = queries.shape[0]
    head_count = queries.shape[1] // HEAD_DIM
    query_heads = queries.reshape(length, head_count, HEAD_DIM)
    key_heads = keys.reshape(length, head_count, HEAD_DIM)
    grad_heads = attn_grad.reshape(length, head_count, HEAD_DIM)
    block_rows = min(256, length)
    score_scale = HEAD_DIM ** (-0.5)
    position = jnp.arange(length)
    result = jnp.zeros((length, head_count, HEAD_DIM), jnp.float32)
    for first_row in range(0, length, block_rows):
        stop_row = first_row + block_rows
        scores = (
            jnp.einsum(
                "qhd,khd->hqk",
                query_heads[first_row:stop_row],
                key_heads[:stop_row],
                preferred_element_type=jnp.float32,
            )
            * score_scale
        )
        allowed = (position[first_row:stop_row, None] >= position[None, :stop_row]) & (
            segment_row[first_row:stop_row, None] == segment_row[None, :stop_row]
        )
        masked = jnp.where(allowed[None], scores, -jnp.inf)
        highest = jnp.max(masked, axis=2, keepdims=True)
        weights = jnp.where(allowed[None], jnp.exp(masked - highest), 0.0)
        probabilities = (weights / jnp.sum(weights, axis=2, keepdims=True)).astype(jnp.bfloat16)
        update = jnp.einsum(
            "hqk,qhd->khd",
            probabilities,
            grad_heads[first_row:stop_row],
            preferred_element_type=jnp.float32,
        )
        result = result.at[:stop_row].add(update)
    return result.reshape(length, head_count * HEAD_DIM).astype(jnp.bfloat16)


def reduce_bucket(term_rows, owned_count):
    return lax.psum_scatter(
        term_rows(jnp.int32(0), owned_count * lax.axis_size("dp")),
        "dp",
        scatter_dimension=0,
        tiled=True,
    )


def shards(d_out, attn_out, queries, keys, out_weight, segment_ids):
    grads_local = d_out[0]
    outputs = attn_out[0]
    owned_count = out_weight.shape[0] // lax.axis_size("dp")
    gathered = lax.all_gather(grads_local, "tensor", axis=0, tiled=True)
    attn_grad = lax.dot_general(
        gathered, out_weight, (((1,), (1,)), ((), ())), preferred_element_type=jnp.float32
    ).astype(jnp.bfloat16)

    def term_rows(start, count):
        return lax.dot_general(
            outputs, gathered, (((0,), (0,)), ((), ())), preferred_element_type=jnp.float32
        )

    value_rows = value_path(queries[0], keys[0], attn_grad, segment_ids[0])
    owned_rows = reduce_bucket(term_rows, owned_count)
    return (value_rows[None], owned_rows / lax.axis_size("dp"))


def solution(mesh):
    placed = (
        P("dp", "tensor", None),
        P("dp", None, "tensor"),
        P("dp", None, "tensor"),
        P("dp", None, "tensor"),
        P("tensor", None),
        P("dp", None),
    )
    return jax.shard_map(
        shards,
        mesh=mesh,
        in_specs=placed,
        out_specs=(P("dp", None, "tensor"), P(("tensor", "dp"), None)),
        check_vma=False,
    )
```

profile of v0, /device:TPU:0, one launch (start us, length us, event | category | flops | bytes accessed | tf_op | source)
XLA Modules:
  0.0 151.6 jit_solution(3062721244602180579)
XLA Ops:
  7.2 0.7 all-gather.3.cloned.1.call-update
  7.9 0.0 reduce-scatter.2.cloned.1.call-start
  8.0 59.2 %all-gather.3.cloned.1.call-done = bf16[1,512,2560]{2,1,0:T(8,128)(2,1)} async-done(((bf16[1,128,2560]{2,1,0:T(8,128)(2,1)}), bf16[1,512,2560]{2,1,0:T(8,128)(2,1)}) %all-gather.3.cloned.1.call-update) | async-done | bytes 2621456 | tf_op jit(solution)/shard_map/all_gather | solution.py:60
  67.1 7.0 %fusion.2 = f32[768,2560]{1,0:T(8,128)} fusion(bf16[1,512,2560]{2,1,0:T(8,128)(2,1)} %all-gather.3.cloned.1.call-done, bf16[1,512,768]{2,1,0:T(8,128)(2,1)S(1)} %copy-done), kind=kOutput, calls=%fused_computation.5 | convolution fusion | flops 2013265920 | bytes 11272192 | tf_op jit(solution)/shard_map/dot_general | solution.py:66
  74.2 1.1 copy-done.3
  75.3 0.3 copy.15
  75.6 0.1 fusion.25
  75.7 0.9 copy.31
  76.6 0.2 copy.30
  76.8 0.1 compare_and_fusion
  77.0 0.8 fusion.17
  77.8 1.9 %fusion.28 = (f32[6,256]{1,0:T(8,128)S(1)}, f32[6,256,256]{1,2,0:T(8,128)}) fusion(bf16[256,6,128]{0,2,1:T(8,128)(2,1)S(1)} %bitcast.39, bf16[256,6,128]{0,2,1:T(8,128)(2,1)S(1)} %bitcast.38, pred[256,256]{0,1:T(8,128)(4,1)S(1)} %compare_and_fusion), kind=kOutput, calls=%fused_computation.36 | convolution fusion | flops 102629632 | bytes 2430976 | tf_op jit(solution)/shard_map/sub | solution.py:35
  79.7 4.9 %fusion.29 = (f32[6,256]{1,0:T(8,128)S(1)}, f32[6,256,512]{2,1,0:T(8,128)}) fusion(pred[256,512]{1,0:T(8,128)(4,1)} %fusion.17, bf16[256,6,128]{0,2,1:T(8,128)(2,1)} %bitcast.37, bf16[512,6,128]{0,2,1:T(8,128)(2,1)} %bitcast.35), kind=kOutput, calls=%fused_computation.37 | convolution fusion | flops 205259264 | bytes 4462592 | tf_op jit(solution)/shard_map/sub | solution.py:35
  84.7 5.0 %fusion.13 = bf16[512,768]{1,0:T(8,128)(2,1)S(1)} fusion(bf16[768,2560]{1,0:T(8,128)(2,1)} %param.16, bf16[1,512,2560]{2,1,0:T(8,128)(2,1)S(1)} %copy-done.1), kind=kOutput, calls=%fused_computation.20 | convolution fusion | flops 2013659136 | bytes 7340032 | tf_op jit(solution)/shard_map/dot_general | solution.py:61
  89.7 0.1 fusion.26
  89.8 0.2 copy.19
  90.0 0.2 copy.13
  90.1 1.0 copy-done.6
  91.2 0.4 convolution_bitcast_fusion
  91.6 1.5 copy-done.7
  93.1 0.5 fusion.8
  93.6 1.2 copy.24
  94.7 47.8 %reduce-scatter.2.cloned.1.call-done = f32[96,2560]{1,0:T(8,128)} async-done(((f32[768,2560]{1,0:T(8,128)}), f32[96,2560]{1,0:T(8,128)}) %reduce-scatter.2.cloned.1.call-update) | async-done | bytes 983056 | tf_op jit(solution)/shard_map/reduce_scatter | solution.py:48
  142.5 2.2 %broadcast_multiply_fusion = f32[96,2560]{1,0:T(8,128)} fusion(f32[96,2560]{1,0:T(8,128)} %reduce-scatter.2.cloned.1.call-done), kind=kLoop, calls=%fused_computation.25 | loop fusion | flops 245760 | bytes 1966080 | tf_op jit(solution)/shard_map/div | solution.py:72
  (21 shorter events, 0.1 us)
Async XLA Ops:
  7.2 60.0 %copy-start = (bf16[1,512,768]{2,1,0:T(8,128)(2,1)S(1)}, bf16[1,512,768]{2,1,0:T(8,128)(2,1)}, u32[]{:S(2)}) copy-start(bf16[1,512,768]{2,1,0:T(8,128)(2,1)} %param.13) | copy-start | bytes 2359300
  7.2 59.9 %all-gather.3.cloned.1.call-start = ((), (), s32[]{:S(2)}) async-start(), calls=%async_computation.2 | async-start | bytes 3276800 | tf_op jit(solution)/shard_map/all_gather | solution.py:60
  7.9 134.6 %reduce-scatter.2.cloned.1.call-start = ((), (), s32[]{:S(2)}) async-start(), calls=%async_computation.1 | async-start | bytes 8847360 | tf_op jit(solution)/shard_map/reduce_scatter | solution.py:48
  74.2 1.1 copy-start.3
  74.2 1.4 copy-start.4
  75.3 1.5 copy-start.5
  75.6 4.2 %copy-start.2 = (bf16[1,512,768]{1,2,0:T(8,128)(2,1)}, bf16[1,512,768]{1,2,0:T(8,128)(2,1)S(1)}, u32[]{:S(2)}) copy-start(bf16[1,512,768]{1,2,0:T(8,128)(2,1)S(1)} %copy.15) | copy-start | bytes 2359300
  79.7 4.9 %copy-start.1 = (bf16[1,512,2560]{2,1,0:T(8,128)(2,1)S(1)}, bf16[1,512,2560]{2,1,0:T(8,128)(2,1)}, u32[]{:S(2)}) copy-start(bf16[1,512,2560]{2,1,0:T(8,128)(2,1)} %all-gather.3.cloned.1.call-done) | copy-start | bytes 7864324
  89.7 1.5 copy-start.6
  91.2 1.9 %copy-start.7 = (f32[6,256,512]{2,1,0:T(8,128)S(1)}, f32[6,256,512]{2,1,0:T(8,128)}, u32[]{:S(2)}) copy-start(f32[6,256,512]{2,1,0:T(8,128)} %get-tuple-element.47) | copy-start | bytes 9437188
Sparse Core Ops, SparseCore 0:
  9.6 57.4 all-gather.2
  74.3 68.1 reduce-scatter.1
where the time goes:
time: 152 us
  waiting for transfers between devices  108 us (71%)
  matrix products  19.9 us (13%)
  between operations  14.2 us (9%)
  local copies, waits for them, and re-layouts  6.61 us (4%)
  other arithmetic  3.19 us (2%)
    all_gather x1, waiting for transfers between devices, shards(): gathered = lax.all_gather(grads_local, 'tensor', axis=0, tiled=True)  59.2 us
    reduce_scatter x1, waiting for transfers between devices, reduce_bucket(): lax.psum_scatter(term_rows(jnp.int32(0), owned_count * lax.axis_size('dp'...  47.8 us
    dot_general x1, matrix products, term_rows(): lax.dot_general(outputs, gathered, (((0,), (0,)), ((), ())), preferred_el...  7.04 us
    sub x2, matrix products, value_path(): weights = jnp.where(allowed[None], jnp.exp(masked - highest), 0.0)  6.87 us
    unnamed x20, local copies, waits for them, and re-layouts  6.12 us
    dot_general x1, matrix products, shards(): lax.dot_general(gathered, out_weight, (((1,), (1,)), ((), ())), preferred...  5.05 us
  transfers between devices with their start and end apart: 2, of which 2 were waited for; matrix products, arithmetic and copies ran while one was open for 11% of the time, Pallas kernels for 0%

commit v1 on v0

--- a/solution.py
+++ b/solution.py
@@ -1,6 +1,10 @@
+import functools
+
 import jax
 import jax.numpy as jnp
 from jax import lax
+from jax.experimental import pallas as pl
+from jax.experimental.pallas import tpu as pltpu
 from jax.sharding import PartitionSpec as P
 
 HEAD_DIM = 128
@@ -53,7 +57,418 @@
     )
 
 
+def fits_kernel(d_out, attn_out, out_weight):
+    dp, tensor = lax.axis_size("dp"), lax.axis_size("tensor")
+    rows, length = d_out.shape[1], attn_out.shape[1]
+    features, width = out_weight.shape
+    return (
+        tensor >= 2
+        and dp % 2 == 0
+        and 4 <= dp <= 16
+        and features % (dp * 16) == 0
+        and features % HEAD_DIM == 0
+        and rows % 16 == 0
+        and length % 128 == 0
+        and length * features * 24 + length * width * 2 + features * width * 7 < 40 * 2**20
+        and width % chunk_width(width) == 0
+        and width // chunk_width(width) >= 3
+    )
+
+
+def chunk_width(width):
+    return 256 if width % 256 == 0 else 128
+
+
+def kernel(
+    dp,
+    tensor,
+    d_out,
+    attn_out,
+    queries,
+    keys,
+    weight,
+    segments,
+    value_out,
+    owned_out,
+    grads,
+    weights,
+    outputs,
+    query_buf,
+    key_buf,
+    segment_buf,
+    turned,
+    flipped,
+    probs,
+    total,
+    pair_send,
+    pair_recv,
+    kept,
+    group_send,
+    group_recv,
+    mine,
+    load_sem,
+    grad_sem,
+    weight_sem,
+    up_send,
+    up_recv,
+    down_send,
+    down_recv,
+    pair_send_sem,
+    pair_recv_sem,
+    group_send_sem,
+    group_recv_sem,
+):
+    chunks, length, width = grads.shape
+    rows = length // tensor
+    features = weight.shape[0]
+    owned = features // dp
+    groups = dp // 2
+    heads = features // HEAD_DIM
+    z = lax.axis_index("tensor")
+    d = lax.axis_index("dp")
+    core = lax.rem(d, 2)
+    group = d // 2
+    sibling = 2 * group + 1 - core
+    last = chunks - 1
+
+    def columns(c):
+        return pl.ds(pl.multiple_of(c * width, width), width)
+
+    def grad_rows(s):
+        return pl.ds(pl.multiple_of(s * rows, rows), rows)
+
+    def block_rows(g):
+        return pl.ds(pl.multiple_of(g * owned, owned), owned)
+
+    def load_grad(c):
+        return pltpu.make_async_copy(
+            d_out.at[0, :, columns(c)], grads.at[c, grad_rows(z), :], grad_sem.at[c]
+        )
+
+    def load_weight(c):
+        return pltpu.make_async_copy(weight.at[:, columns(c)], weights.at[c], weight_sem.at[c])
+
+    loads = [
+        pltpu.make_async_copy(segments, segment_buf, load_sem.at[0]),
+        pltpu.make_async_copy(queries.at[0], query_buf, load_sem.at[1]),
+        pltpu.make_async_copy(keys.at[0], key_buf, load_sem.at[2]),
+        pltpu.make_async_copy(attn_out.at[0], outputs, load_sem.at[3]),
+    ]
+
+    def start_grad(c, carry):
+        load_grad(c).start()
+        return carry
+
+    def start_weight(c, carry):
+        load_weight(c).start()
+        return carry
+
+    lax.fori_loop(0, chunks, start_grad, 0)
+    for load in loads:
+        load.start()
+    lax.fori_loop(0, chunks, start_weight, 0)
+
+    barrier = pltpu.get_barrier_semaphore()
+
+    @pl.when(z > 0)
+    def _():
+        pl.semaphore_signal(barrier, inc=1, device_id={"tensor": z - 1}, device_id_type=pl.DeviceIdType.MESH)
+
+    @pl.when(z < tensor - 1)
+    def _():
+        pl.semaphore_signal(barrier, inc=1, device_id={"tensor": z + 1}, device_id_type=pl.DeviceIdType.MESH)
+
+    pl.semaphore_signal(barrier, inc=1, device_id={"dp": sibling}, device_id_type=pl.DeviceIdType.MESH)
+    for step in range(1, groups):
+        peer = 2 * lax.rem(group + step, groups) + core
+        pl.semaphore_signal(barrier, inc=1, device_id={"dp": peer}, device_id_type=pl.DeviceIdType.MESH)
+
+    pl.semaphore_wait(barrier, groups + jnp.minimum(z, 1) + jnp.minimum(tensor - 1 - z, 1))
+
+    def up(c, hop):
+        piece = grads.at[c, grad_rows(z - hop), :]
+        return pltpu.make_async_remote_copy(
+            src_ref=piece,
+            dst_ref=piece,
+            send_sem=up_send.at[hop, c],
+            recv_sem=up_recv.at[hop, c],
+            device_id={"tensor": z + 1},
+            device_id_type=pl.DeviceIdType.MESH,
+        )
+
+    def down(c, hop):
+        piece = grads.at[c, grad_rows(z + hop), :]
+        return pltpu.make_async_remote_copy(
+            src_ref=piece,
+            dst_ref=piece,
+            send_sem=down_send.at[hop, c],
+            recv_sem=down_recv.at[hop, c],
+            device_id={"tensor": z - 1},
+            device_id_type=pl.DeviceIdType.MESH,
+        )
+
+    def arrived_up(c, hop):
+        piece = grads.at[c, grad_rows(z - hop - 1), :]
+        return pltpu.make_async_remote_copy(
+            src_ref=piece,
+            dst_ref=piece,
+            send_sem=up_send.at[hop, c],
+            recv_sem=up_recv.at[hop, c],
+            device_id={"tensor": z - 1},
+            device_id_type=pl.DeviceIdType.MESH,
+        )
+
+    def arrived_down(c, hop):
+        piece = grads.at[c, grad_rows(z + hop + 1), :]
+        return pltpu.make_async_remote_copy(
+            src_ref=piece,
+            dst_ref=piece,
+            send_sem=down_send.at[hop, c],
+            recv_sem=down_recv.at[hop, c],
+            device_id={"tensor": z + 1},
+            device_id_type=pl.DeviceIdType.MESH,
+        )
+
+    def send(c, hop):
+        @pl.when((z - hop >= 0) & (z < tensor - 1))
+        def _():
+            up(c, hop).start()
+
+        @pl.when((z + hop < tensor) & (z > 0))
+        def _():
+            down(c, hop).start()
+
+    def send_own(c):
+        load_grad(c).wait()
+        send(c, 0)
+
+    def receive(c, hop):
+        @pl.when(z - hop - 1 >= 0)
+        def _():
+            arrived_up(c, hop).wait_recv()
+            if hop + 1 < tensor - 1:
+
+                @pl.when(z < tensor - 1)
+                def _():
+                    up(c, hop + 1).start()
+
+        @pl.when(z + hop + 1 < tensor)
+        def _():
+            arrived_down(c, hop).wait_recv()
+            if hop + 1 < tensor - 1:
+
+                @pl.when(z > 0)
+                def _():
+                    down(c, hop + 1).start()
+
+    def pair_copy(c):
+        return pltpu.make_async_remote_copy(
+            src_ref=pair_send.at[c],
+            dst_ref=pair_recv.at[c],
+            send_sem=pair_send_sem.at[c],
+            recv_sem=pair_recv_sem.at[c],
+            device_id={"dp": sibling},
+            device_id_type=pl.DeviceIdType.MESH,
+        )
+
+    def group_copy(c, step):
+        peer = 2 * lax.rem(group + step, groups) + core
+        return pltpu.make_async_remote_copy(
+            src_ref=group_send.at[c, step - 1],
+            dst_ref=group_recv.at[c, step - 1],
+            send_sem=group_send_sem.at[c, step - 1],
+            recv_sem=group_recv_sem.at[c, step - 1],
+            device_id={"dp": peer},
+            device_id_type=pl.DeviceIdType.MESH,
+        )
+
+    ahead = min(2, chunks)
+    for c in range(ahead):
+        send_own(c)
+
+    for load in loads:
+        load.wait()
+    turned[...] = outputs[...].T
+    for part in range(2):
+        owner_core = 1 - core if part == 0 else core
+        for g in range(groups):
+            flipped[part, g * owned : (g + 1) * owned, :] = turned[block_rows(2 * g + owner_core), :]
+    total[...] = jnp.zeros_like(total)
+
+    block = min(256, length)
+    ids = segment_buf[...].astype(jnp.float32)
+    ids_down = jnp.broadcast_to(ids, (128, length)).T[:, :1]
+
+    def head_probs(h):
+        at = pl.ds(pl.multiple_of(h * HEAD_DIM, HEAD_DIM), HEAD_DIM)
+        for first in range(0, length, block):
+            stop = first + block
+            scores = lax.dot_general(
+                key_buf[:stop, at],
+                query_buf[first:stop, at],
+                (((1,), (1,)), ((), ())),
+                preferred_element_type=jnp.float32,
+            ) * (HEAD_DIM ** (-0.5))
+            key_at = lax.broadcasted_iota(jnp.int32, (stop, block), 0)
+            query_at = first + lax.broadcasted_iota(jnp.int32, (stop, block), 1)
+            allowed = (key_at <= query_at) & (ids_down[:stop] == ids[:, first:stop])
+            masked = jnp.where(allowed, scores, -jnp.inf)
+            highest = jnp.max(masked, axis=0, keepdims=True)
+            terms = jnp.exp(masked - highest)
+            probs[h, :stop, first:stop] = (
+                terms * (1.0 / jnp.sum(terms, axis=0, keepdims=True))
+            ).astype(jnp.bfloat16)
+
+    def multiply(c):
+        load_weight(c).wait()
+        grad = grads[c]
+        pair_send[c] = jnp.dot(flipped[0], grad, preferred_element_type=jnp.float32).astype(jnp.bfloat16)
+        pair_copy(c).start()
+        kept[c] = jnp.dot(flipped[1], grad, preferred_element_type=jnp.float32)
+        total[...] += lax.dot_general(
+            grad, weights[c], (((1,), (1,)), ((), ())), preferred_element_type=jnp.float32
+        )
+
+    def combine(c):
+        pair_copy(c).wait_recv()
+        for step in range(1, groups):
+            at = block_rows(lax.rem(group + step, groups))
+            group_send[c, step - 1] = (kept[c, at, :] + pair_recv[c, at, :].astype(jnp.float32)).astype(jnp.bfloat16)
+            group_copy(c, step).start()
+        at = block_rows(group)
+        mine[c] = kept[c, at, :] + pair_recv[c, at, :].astype(jnp.float32)
+
+    def finish(c):
+        result = mine[c]
+        for step in range(1, groups):
+            group_copy(c, step).wait_recv()
+            result += group_recv[c, step - 1].astype(jnp.float32)
+        owned_out[:, columns(c)] = result / dp
+
+    lag = tensor - 2
+
+    def turn(k, carry):
+        @pl.when(k + ahead < chunks)
+        def _():
+            send_own(k + ahead)
+
+        @pl.when(k < heads)
+        def _():
+            head_probs(k)
+
+        for hop in range(tensor - 1):
+            c = k - hop
+
+            @pl.when((c >= 0) & (c < chunks))
+            def _():
+                receive(c, hop)
+
+        @pl.when(k - lag >= 0)
+        def _():
+            multiply(k - lag)
+
+        @pl.when(k - lag - 1 >= 0)
+        def _():
+            combine(k - lag - 1)
+
+        @pl.when(k - lag - 2 >= 0)
+        def _():
+            finish(k - lag - 2)
+
+        return carry
+
+    lax.fori_loop(0, chunks + lag, turn, 0)
+    for h in range(chunks + lag, heads):
+        head_probs(h)
+    combine(last)
+    for h in range(heads):
+        at = slice(h * HEAD_DIM, (h + 1) * HEAD_DIM)
+        for first in range(0, length, block):
+            value_out[0, first : first + block, at] = jnp.dot(
+                probs[h, first : first + block, first:],
+                total[first:, at].astype(jnp.bfloat16),
+                preferred_element_type=jnp.float32,
+            ).astype(jnp.bfloat16)
+    finish(last - 1)
+    finish(last)
+
+    def sent(c, carry):
+        for hop in range(tensor - 1):
+
+            @pl.when((z - hop >= 0) & (z < tensor - 1))
+            def _():
+                up(c, hop).wait_send()
+
+            @pl.when((z + hop < tensor) & (z > 0))
+            def _():
+                down(c, hop).wait_send()
+
+        pair_copy(c).wait_send()
+        for step in range(1, groups):
+            group_copy(c, step).wait_send()
+        return carry
+
+    lax.fori_loop(0, chunks, sent, 0)
+
+
+def fused(d_out, attn_out, queries, keys, out_weight, segment_ids):
+    dp, tensor = lax.axis_size("dp"), lax.axis_size("tensor")
+    length = attn_out.shape[1]
+    features, full = out_weight.shape
+    width = chunk_width(full)
+    chunks = full // width
+    groups = dp // 2
+    owned = features // dp
+    half = features // 2
+    heads = features // HEAD_DIM
+    bf16, f32 = jnp.bfloat16, jnp.float32
+    dma = pltpu.SemaphoreType.DMA
+    return pl.pallas_call(
+        functools.partial(kernel, dp, tensor),
+        out_shape=(
+            jax.ShapeDtypeStruct((1, length, features), bf16),
+            jax.ShapeDtypeStruct((owned, full), f32),
+        ),
+        in_specs=[pl.BlockSpec(memory_space=pl.ANY)] * 6,
+        out_specs=(pl.BlockSpec(memory_space=pltpu.VMEM), pl.BlockSpec(memory_space=pltpu.VMEM)),
+        scratch_shapes=[
+            pltpu.VMEM((chunks, length, width), bf16),
+            pltpu.VMEM((chunks, features, width), bf16),
+            pltpu.VMEM((length, features), bf16),
+            pltpu.VMEM((length, features), bf16),
+            pltpu.VMEM((length, features), bf16),
+            pltpu.VMEM((1, length), jnp.int32),
+            pltpu.VMEM((features, length), bf16),
+            pltpu.VMEM((2, half, length), bf16),
+            pltpu.VMEM((heads, length, length), bf16),
+            pltpu.VMEM((length, features), f32),
+            pltpu.VMEM((chunks, half, width), bf16),
+            pltpu.VMEM((chunks, half, width), bf16),
+            pltpu.VMEM((chunks, half, width), f32),
+            pltpu.VMEM((chunks, groups - 1, owned, width), bf16),
+            pltpu.VMEM((chunks, groups - 1, owned, width), bf16),
+            pltpu.VMEM((chunks, owned, width), f32),
+            dma((4,)),
+            dma((chunks,)),
+            dma((chunks,)),
+            dma((tensor - 1, chunks)),
+            dma((tensor - 1, chunks)),
+            dma((tensor - 1, chunks)),
+            dma((tensor - 1, chunks)),
+            dma((chunks,)),
+            dma((chunks,)),
+            dma((chunks, groups - 1)),
+            dma((chunks, groups - 1)),
+        ],
+        compiler_params=pltpu.CompilerParams(
+            collective_id=0, has_side_effects=True, vmem_limit_bytes=56 * 2**20
+        ),
+    )(d_out, attn_out, queries, keys, out_weight, segment_ids)
+
+
 def shards(d_out, attn_out, queries, keys, out_weight, segment_ids):
+    if fits_kernel(d_out, attn_out, out_weight):
+        return fused(d_out, attn_out, queries, keys, out_weight, segment_ids)
     grads_local = d_out[0]
     outputs = attn_out[0]
     owned_count = out_weight.shape[0] // lax.axis_size("dp")

time: 152 us -> 66.6 us (0.44)
  waiting for transfers between devices: 108 us -> 0 us
  Pallas kernels: 0 us -> 61.5 us
  matrix products: 19.9 us -> 0 us
  between operations: 14.2 us -> 0.64 us
  other arithmetic: 3.19 us -> 0 us
  local copies, waits for them, and re-layouts: 6.61 us -> 4.27 us
    pallas_call x0 -> x1, Pallas kernels: none -> 61.5 us  [fused(): pl.pallas_call(functools.partial(kernel, dp, tensor), out_shape=(jax.Shap...]
    all_gather x1 -> x0, waiting for transfers between devices: 59.2 us -> none  [shards(): gathered = lax.all_gather(grads_local, 'tensor', axis=0, tiled=True)]
    reduce_scatter x1 -> x0, waiting for transfers between devices: 47.8 us -> none  [reduce_bucket(): lax.psum_scatter(term_rows(jnp.int32(0), owned_count * lax.axis_size('dp'...]
    dot_general x4 -> x0, matrix products: 13 us -> none  [the longest x1 7.04 us: term_rows(): lax.dot_general(outputs, gathered, (((0,), (0,)), ((), ())), preferred_el...]
    sub x2 -> x0, matrix products: 6.87 us -> none  [value_path(): weights = jnp.where(allowed[None], jnp.exp(masked - highest), 0.0)]
    div x1 -> x0, other arithmetic: 2.22 us -> none  [shards(): return (value_rows[None], owned_rows / lax.axis_size('dp'))]
    unnamed x20 -> x2, local copies, waits for them, and re-layouts: 6.12 us -> 4.27 us
  transfers between devices with their start and end apart: 2 -> 0, of which waited for: 2 -> 0; matrix products, arithmetic and copies ran while one was open for 11% -> 0% of each run, Pallas kernels for 0% -> 0%
where the time goes in v1:
time: 66.6 us; the launch traced here: 66.4 us
  Pallas kernels  61.5 us (92%)
  local copies, waits for them, and re-layouts  4.27 us (6%)
    pallas_call x1, Pallas kernels, fused(): pl.pallas_call(functools.partial(kernel, dp, tensor), out_shape=(jax.Shap...  61.5 us
    unnamed x2, local copies, waits for them, and re-layouts  4.27 us

profile of v1, /device:TPU:0, one launch (start us, length us, event | category | flops | bytes accessed | tf_op | source)
XLA Modules:
  0.0 66.4 jit_solution(10083048161721265056)
XLA Ops:
  0.6 61.5 %shard_map.77 = (bf16[1,512,768]{2,1,0:T(8,128)(2,1)}, f32[96,2560]{1,0:T(8,128)}) custom-call(bf16[1,128,2560]{2,1,0:T(8,128)(2,1)} %d_out.1, bf16[1,512,768]{2,1,0:T(8,128)(2,1)} %attn_out.1, bf16[1,512,768]{2,1,0:T(8,128)(2,1)} %queries.1, bf16[1,512,768]{2,1,0:T(8,128)(2,1)} %keys.1, bf16[768,2560]{1,0:T(8,128)(2,1)} %weight.1, s32[1,512]{1,0:T(1,128)} %segments.1), custom_call_target="tpu_custom_call" | custom-call | tf_op jit(solution)/shard_map/pallas_call | solution.py:426
  62.1 2.1 %copy.10 = bf16[1,512,768]{2,1,0:T(8,128)(2,1)} copy(bf16[1,512,768]{2,1,0:T(8,128)(2,1)} %get-tuple-element.4) | data formatting | bytes 1572864
  64.2 2.2 %copy.11 = f32[96,2560]{1,0:T(8,128)} copy(f32[96,2560]{1,0:T(8,128)} %get-tuple-element.5) | data formatting | bytes 1966080

commit v2 on v1

--- a/solution.py
+++ b/solution.py
@@ -163,11 +163,6 @@
         load_weight(c).start()
         return carry
 
-    lax.fori_loop(0, chunks, start_grad, 0)
-    for load in loads:
-        load.start()
-    lax.fori_loop(0, chunks, start_weight, 0)
-
     barrier = pltpu.get_barrier_semaphore()
 
     @pl.when(z > 0)
@@ -188,7 +183,7 @@
     def up(c, hop):
         piece = grads.at[c, grad_rows(z - hop), :]
         return pltpu.make_async_remote_copy(
-            src_ref=piece,
+            src_ref=d_out.at[0, :, columns(c)] if hop == 0 else piece,
             dst_ref=piece,
             send_sem=up_send.at[hop, c],
             recv_sem=up_recv.at[hop, c],
@@ -199,7 +194,7 @@
     def down(c, hop):
         piece = grads.at[c, grad_rows(z + hop), :]
         return pltpu.make_async_remote_copy(
-            src_ref=piece,
+            src_ref=d_out.at[0, :, columns(c)] if hop == 0 else piece,
             dst_ref=piece,
             send_sem=down_send.at[hop, c],
             recv_sem=down_recv.at[hop, c],
@@ -239,7 +234,6 @@
             down(c, hop).start()
 
     def send_own(c):
-        load_grad(c).wait()
         send(c, 0)
 
     def receive(c, hop):
@@ -282,10 +276,14 @@
             device_id_type=pl.DeviceIdType.MESH,
         )
 
-    ahead = min(2, chunks)
+    ahead = min(3, chunks)
     for c in range(ahead):
         send_own(c)
 
+    for load in loads:
+        load.start()
+    lax.fori_loop(0, chunks, start_grad, 0)
+    lax.fori_loop(0, chunks, start_weight, 0)
     for load in loads:
         load.wait()
     turned[...] = outputs[...].T
@@ -321,6 +319,7 @@
 
     def multiply(c):
         load_weight(c).wait()
+        load_grad(c).wait()
         grad = grads[c]
         pair_send[c] = jnp.dot(flipped[0], grad, preferred_element_type=jnp.float32).astype(jnp.bfloat16)
         pair_copy(c).start()
@@ -348,14 +347,6 @@
     lag = tensor - 2
 
     def turn(k, carry):
-        @pl.when(k + ahead < chunks)
-        def _():
-            send_own(k + ahead)
-
-        @pl.when(k < heads)
-        def _():
-            head_probs(k)
-
         for hop in range(tensor - 1):
             c = k - hop
 
@@ -363,6 +354,10 @@
             def _():
                 receive(c, hop)
 
+        @pl.when(k + ahead < chunks)
+        def _():
+            send_own(k + ahead)
+
         @pl.when(k - lag >= 0)
         def _():
             multiply(k - lag)
@@ -371,9 +366,13 @@
         def _():
             combine(k - lag - 1)
 
-        @pl.when(k - lag - 2 >= 0)
-        def _():
-            finish(k - lag - 2)
+        @pl.when(k - lag - 3 >= 0)
+        def _():
+            finish(k - lag - 3)
+
+        @pl.when(k < heads)
+        def _():
+            head_probs(k)
 
         return carry
 
@@ -389,6 +388,7 @@
                 total[first:, at].astype(jnp.bfloat16),
                 preferred_element_type=jnp.float32,
             ).astype(jnp.bfloat16)
+    finish(last - 2)
     finish(last - 1)
     finish(last)
 
@@ -409,6 +409,47 @@
         return carry
 
     lax.fori_loop(0, chunks, sent, 0)
+
+
+def hand_on(values, sums, value_out, owned_out, value_buf, owned_buf, load_sem, store_sem):
+    parts = load_sem.shape[1]
+    loads, stores = [], []
+    for index, (source, middle, target, dim) in enumerate(
+        ((values, value_buf, value_out, 1), (sums, owned_buf, owned_out, 0))
+    ):
+        step = source.shape[dim] // parts
+        for part in range(parts):
+            at = (slice(None),) * dim + (pl.ds(part * step, step),)
+            loads.append(pltpu.make_async_copy(source.at[at], middle.at[at], load_sem.at[index, part]))
+            stores.append(pltpu.make_async_copy(middle.at[at], target.at[at], store_sem.at[index, part]))
+    for load in loads:
+        load.start()
+    for load, store in zip(loads, stores):
+        load.wait()
+        store.start()
+    for store in stores:
+        store.wait()
+
+
+def deliver(values, sums):
+    parts = 2 if values.shape[1] % 32 == 0 and sums.shape[0] % 16 == 0 else 1
+    dma = pltpu.SemaphoreType.DMA
+    return pl.pallas_call(
+        hand_on,
+        out_shape=(
+            jax.ShapeDtypeStruct(values.shape, values.dtype),
+            jax.ShapeDtypeStruct(sums.shape, sums.dtype),
+        ),
+        in_specs=[pl.BlockSpec(memory_space=pl.ANY)] * 2,
+        out_specs=(pl.BlockSpec(memory_space=pl.ANY),) * 2,
+        scratch_shapes=[
+            pltpu.VMEM(values.shape, values.dtype),
+            pltpu.VMEM(sums.shape, sums.dtype),
+            dma((2, parts)),
+            dma((2, parts)),
+        ],
+        compiler_params=pltpu.CompilerParams(vmem_limit_bytes=60 * 2**20),
+    )(values, sums)
 
 
 def fused(d_out, attn_out, queries, keys, out_weight, segment_ids):
@@ -423,7 +464,7 @@
     heads = features // HEAD_DIM
     bf16, f32 = jnp.bfloat16, jnp.float32
     dma = pltpu.SemaphoreType.DMA
-    return pl.pallas_call(
+    values, sums = pl.pallas_call(
         functools.partial(kernel, dp, tensor),
         out_shape=(
             jax.ShapeDtypeStruct((1, length, features), bf16),
@@ -464,6 +505,7 @@
             collective_id=0, has_side_effects=True, vmem_limit_bytes=56 * 2**20
         ),
     )(d_out, attn_out, queries, keys, out_weight, segment_ids)
+    return deliver(values, sums)
 
 
 def shards(d_out, attn_out, queries, keys, out_weight, segment_ids):

time: 66.6 us -> 62.8 us (0.943)
  local copies, waits for them, and re-layouts: 4.27 us -> 0 us
    unnamed x2 -> x0, local copies, waits for them, and re-layouts: 4.27 us -> none
    pallas_call x0 -> x1, Pallas kernels: none -> 2.28 us  [deliver(): pl.pallas_call(hand_on, out_shape=(jax.ShapeDtypeStruct(values.shape, val...]
    pallas_call x1, Pallas kernels: 61.5 us -> 59.8 us  [fused(): pl.pallas_call(functools.partial(kernel, dp, tensor), out_shape=(jax.Shap...]
where the time goes in v2:
time: 62.8 us; the launch traced here: 62.7 us
  Pallas kernels  62 us (99%)
  between operations  0.64 us (1%)
    pallas_call x1, Pallas kernels, fused(): pl.pallas_call(functools.partial(kernel, dp, tensor), out_shape=(jax.Shap...  59.8 us
    pallas_call x1, Pallas kernels, deliver(): pl.pallas_call(hand_on, out_shape=(jax.ShapeDtypeStruct(values.shape, val...  2.28 us

profile of v2, /device:TPU:0, one launch (start us, length us, event | category | flops | bytes accessed | tf_op | source)
XLA Modules:
  0.0 62.7 jit_solution(1174845199004456556)
XLA Ops:
  0.6 59.8 %shard_map.77 = (bf16[1,512,768]{2,1,0:T(8,128)(2,1)}, f32[96,2560]{1,0:T(8,128)}) custom-call(bf16[1,128,2560]{2,1,0:T(8,128)(2,1)} %d_out.1, bf16[1,512,768]{2,1,0:T(8,128)(2,1)} %attn_out.1, bf16[1,512,768]{2,1,0:T(8,128)(2,1)} %queries.1, bf16[1,512,768]{2,1,0:T(8,128)(2,1)} %keys.1, bf16[768,2560]{1,0:T(8,128)(2,1)} %weight.1, s32[1,512]{1,0:T(1,128)} %segments.1), custom_call_target="tpu_custom_call" | custom-call | tf_op jit(solution)/shard_map/pallas_call | solution.py:467
  60.4 2.3 %shard_map.78 = (bf16[1,512,768]{2,1,0:T(8,128)(2,1)}, f32[96,2560]{1,0:T(8,128)}) custom-call(bf16[1,512,768]{2,1,0:T(8,128)(2,1)} %get-tuple-element.4.values, f32[96,2560]{1,0:T(8,128)} %get-tuple-element.5.sums), custom_call_target="tpu_custom_call" | custom-call | tf_op jit(solution)/shard_map/pallas_call | solution.py:437
